TPU v7x, 128 devices: a whole 4x4x4 slice. The times are simulated.
128 devices in a mesh: cluster: 8 (over z, x_hi), dp: 16 (over y, x_lo, core).
Axes of the slice: x: 4 (x_hi: 2, x_lo: 2; x = x_hi * 2 + x_lo), y: 4, z: 4, core: 2. Of those that a mesh axis runs over, the one named last changes fastest.
Arguments:
- documents: bfloat16 [32768, 1024], P('dp', 'cluster'), may hold values from -64 to 64
- centroids: bfloat16 [16384, 1024], P('cluster'), may hold values from -8 to 8
- domain_mass: float32 [32768, 256], P('dp'), may hold values from 0.01 to 10
Outputs:
- lift: float32 [16384, 256], P(('cluster', 'dp'))
- information: float32 [], replicated
All inputs are finite; a program needn't handle non-finite values.
Results may differ from a plain program's by a relative error of at most 0.0013.
Values may be sent and summed in bfloat16 or wider, within the bound.
A program may use at most 128 MiB of HBM per device.

v0:
```python
import math
import jax
import jax.numpy as jnp
from jax import lax
from jax.sharding import PartitionSpec as P

E = 1024


def shards(documents, centroids, domain_mass):
    scale = 3.0 / math.sqrt(E)
    doc_rows = documents.shape[0]
    local_k = centroids.shape[0]
    docs_total = doc_rows * lax.axis_size("dp")
    own_rows = local_k // lax.axis_size("dp")
    columns = centroids
    scores = (
        lax.dot_general(
            lax.all_gather(documents, "cluster", axis=1, tiled=True),
            columns,
            (((1,), (1,)), ((), ())),
            preferred_element_type=jnp.float32,
        )
        * scale
    )
    row_max = lax.pmax(jnp.max(scores, axis=1), "cluster")
    expo = jnp.exp(scores - row_max[:, None])
    row_total = lax.psum(jnp.sum(expo, axis=1), "cluster")
    assign = (expo / row_total[:, None]).astype(jnp.bfloat16)
    shares = (domain_mass / jnp.sum(domain_mass, axis=1, keepdims=True)).astype(jnp.bfloat16)
    columns = assign
    whole = lax.psum(
        lax.dot_general(
            columns, shares, (((0,), (0,)), ((), ())), preferred_element_type=jnp.float32
        ),
        "dp",
    )
    summed = lax.dynamic_slice_in_dim(whole, lax.axis_index("dp") * own_rows, own_rows, 0)
    joint = summed / docs_total
    cluster_mass = jnp.sum(joint, axis=1)
    domain_prior = lax.psum(jnp.sum(joint, axis=0), ("cluster", "dp"))
    lift = joint / (cluster_mass[:, None] * domain_prior[None, :])
    information = lax.psum(jnp.sum(joint * jnp.log(lift)), ("cluster", "dp"))
    return (lift, information)


def solution(mesh):
    return jax.shard_map(
        shards,
        mesh=mesh,
        in_specs=(P("dp", "cluster"), P("cluster", None), P("dp", None)),
        out_specs=(P(("cluster", "dp"), None), P()),
        check_vma=False,
    )
```

profile of v0, /device:TPU:1, one launch (start us, length us, event | category | flops | bytes accessed | tf_op | source)
XLA Modules:
  0.0 423.9 jit_solution(605599507388424641)
XLA Ops:
  7.2 0.0 all-gather.2.cloned.1.call-start
  7.2 0.7 all-gather.2.cloned.1.call-update
  7.9 0.0 all-reduce.2.cloned.1.call-start
  7.9 1.9 reduce_sum.46
  9.9 77.0 %all-gather.2.cloned.1.call-done = bf16[2048,1024]{1,0:T(8,128)(2,1)} async-done(((bf16[2048,128]{1,0:T(8,128)(2,1)}), bf16[2048,1024]{1,0:T(8,128)(2,1)}) %all-gather.2.cloned.1.call-update) | async-done | bytes 4194320 | tf_op jit(solution)/shard_map/all_gather | solution.py:19
  86.9 15.1 %multiply_reduce_fusion = (f32[2048]{0:T(1024)S(1)}, f32[2048,2048]{0,1:T(8,128)}) fusion(bf16[2048,1024]{1,0:T(8,128)(2,1)} %all-gather.2.cloned.1.call-done, bf16[2048,1024]{1,0:T(8,128)(2,1)} %param.4), kind=kOutput, calls=%fused_computation.2 | convolution fusion | flops 8598321152 | bytes 25174016 | tf_op jit(solution)/shard_map/dot_general | solution.py:18
  102.0 16.6 %pmax.7 = f32[2048]{0:T(1024)S(1)} all-reduce(f32[2048]{0:T(1024)S(1)} %get-tuple-element.6), channel_id=1, replica_groups=mesh['cluster'=8,'dp'=16] {'cluster'}, use_global_device_ids=true, to_apply=%region_1.0 | all-reduce | flops 2048 | bytes 16384 | tf_op jit(solution)/shard_map/pmax | solution.py:26
  118.6 0.0 copy-start
  118.6 8.7 %fusion = f32[2048]{0:T(1024)S(1)} fusion(f32[2048,2048]{0,1:T(8,128)} %get-tuple-element.7, f32[2048]{0:T(1024)S(1)} %pmax.7), kind=kLoop, calls=%fused_computation.3 | loop fusion | flops 12580864 | bytes 16793600 | tf_op jit(solution)/shard_map/reduce_sum | solution.py:28
  127.3 18.2 %psum.28 = f32[2048]{0:T(1024)S(1)} all-reduce(f32[2048]{0:T(1024)S(1)} %fusion), channel_id=1, replica_groups=mesh['cluster'=8,'dp'=16] {'cluster'}, use_global_device_ids=true, to_apply=%region_3.0 | all-reduce | flops 2048 | bytes 16384 | tf_op jit(solution)/shard_map/psum | solution.py:28
  145.5 0.0 copy-done
  145.5 9.1 %fusion.1 = f32[2048,256]{1,0:T(8,128)} fusion(f32[2048,2048]{0,1:T(8,128)} %get-tuple-element.7, f32[2048]{0:T(1024)S(1)} %psum.28, f32[2048]{0:T(1024)S(1)} %pmax.7, f32[2048,256]{1,0:T(8,128)S(1)} %copy-done, f32[2048]{0:T(1024)S(1)} %reduce_sum.46), kind=kOutput, calls=%fused_computation.4 | convolution fusion | flops 2165309440 | bytes 20996096 | tf_op jit(solution)/shard_map/dot_general | solution.py:33
  154.6 0.0 all-reduce.2.cloned.1.call-update
  154.7 129.3 %all-reduce.2.cloned.1.call-done = f32[2048,256]{1,0:T(8,128)} async-done(((f32[2048,256]{1,0:T(8,128)}), f32[2048,256]{1,0:T(8,128)}) %all-reduce.2.cloned.1.call-update) | async-done | bytes 2097168 | tf_op jit(solution)/shard_map/psum | solution.py:32
  283.9 1.0 fusion.4
  284.9 67.3 %psum.30 = f32[256]{0:T(256)S(1)} all-reduce(f32[256]{0:T(256)S(1)} %get-tuple-element.3), channel_id=1, replica_groups=mesh['cluster'=8,'dp'=16] {'cluster','dp'}, use_global_device_ids=true, to_apply=%region_8.0 | all-reduce | flops 256 | bytes 2048 | tf_op jit(solution)/shard_map/psum | solution.py:41
  352.2 2.3 multiply_reduce_fusion.1
  354.5 62.6 %psum.31 = f32[]{:T(128)} all-reduce(f32[]{:T(128)} %get-tuple-element.4), channel_id=1, replica_groups=mesh['cluster'=8,'dp'=16] {'cluster','dp'}, use_global_device_ids=true, to_apply=%region_10.0 | all-reduce | flops 1 | bytes 8 | tf_op jit(solution)/shard_map/psum | solution.py:43
Async XLA Ops:
  7.2 79.7 %all-gather.2.cloned.1.call-start = ((), (), s32[]{:S(2)}) async-start(), calls=%async_computation | async-start | bytes 4718592 | tf_op jit(solution)/shard_map/all_gather | solution.py:19
  7.9 276.0 %all-reduce.2.cloned.1.call-start = ((), (), s32[]{:S(2)}) async-start(), calls=%async_computation.1 | async-start | bytes 4194304 | tf_op jit(solution)/shard_map/psum | solution.py:32
  118.6 26.9 %copy-start = (f32[2048,256]{1,0:T(8,128)S(1)}, f32[2048,256]{1,0:T(8,128)}, u32[]{:S(2)}) copy-start(f32[2048,256]{1,0:T(8,128)} %param.5) | copy-start | bytes 6291460
Sparse Core Ops, SparseCore 0:
  10.2 76.6 all-gather.1
  154.8 129.0 all-reduce.1
where the time goes:
time: 424 us
  waiting for transfers between devices  207 us (49%)
  blocking collectives  165 us (39%)
  matrix products  24.2 us (6%)
  between operations  14.1 us (3%)
  other arithmetic  13.9 us (3%)
    psum x1, waiting for transfers between devices, shards(): lax.psum(lax.dot_general(columns, shares, (((0,), (0,)), ((), ())), prefe...  129 us
    all_gather x1, waiting for transfers between devices, shards(): lax.all_gather(documents, 'cluster', axis=1, tiled=True)  77 us
    psum x1, blocking collectives, shards(): domain_prior = lax.psum(jnp.sum(joint, axis=0), ('cluster', 'dp'))  67.3 us
    psum x1, blocking collectives, shards(): information = lax.psum(jnp.sum(joint * jnp.log(lift)), ('cluster', 'dp'))  62.6 us
    psum x1, blocking collectives, shards(): row_total = lax.psum(jnp.sum(expo, axis=1), 'cluster')  18.2 us
    pmax x1, blocking collectives, shards(): row_max = lax.pmax(jnp.max(scores, axis=1), 'cluster')  16.6 us
    dot_general x1, matrix products, shards(): lax.dot_general(lax.all_gather(documents, 'cluster', axis=1, tiled=True),...  15.1 us
    dot_general x1, matrix products, shards(): lax.dot_general(columns, shares, (((0,), (0,)), ((), ())), preferred_elem...  9.11 us
  transfers between devices with their start and end apart: 2, of which 2 were waited for; matrix products, arithmetic and copies ran while one was open for 0% of the time, Pallas kernels for 0%

commit v1 on v0

--- a/solution.py
+++ b/solution.py
@@ -38,7 +38,7 @@
     summed = lax.dynamic_slice_in_dim(whole, lax.axis_index("dp") * own_rows, own_rows, 0)
     joint = summed / docs_total
     cluster_mass = jnp.sum(joint, axis=1)
-    domain_prior = lax.psum(jnp.sum(joint, axis=0), ("cluster", "dp"))
+    domain_prior = lax.psum(lax.psum(jnp.sum(joint, axis=0), "dp"), "cluster")
     lift = joint / (cluster_mass[:, None] * domain_prior[None, :])
     information = lax.psum(jnp.sum(joint * jnp.log(lift)), ("cluster", "dp"))
     return (lift, information)

time: 424 us -> 412 us (0.972)
  blocking collectives: 165 us -> 152 us
    psum x1 -> x2, blocking collectives: 67.3 us -> 48.6 us  [shards(): domain_prior = lax.psum(lax.psum(jnp.sum(joint, axis=0), 'dp'), 'cluster')]
    psum x1, blocking collectives: 62.6 us -> 68.6 us  [shards(): information = lax.psum(jnp.sum(joint * jnp.log(lift)), ('cluster', 'dp'))]
where the time goes in v1:
time: 412 us; the launch traced here: 411 us
  waiting for transfers between devices  207 us (50%)
  blocking collectives  152 us (37%)
  matrix products  24.2 us (6%)
  between operations  14.1 us (3%)
  other arithmetic  13.9 us (3%)
    psum x1, waiting for transfers between devices, shards(): lax.psum(lax.dot_general(columns, shares, (((0,), (0,)), ((), ())), prefe...  129 us
    all_gather x1, waiting for transfers between devices, shards(): lax.all_gather(documents, 'cluster', axis=1, tiled=True)  77 us
    psum x1, blocking collectives, shards(): information = lax.psum(jnp.sum(joint * jnp.log(lift)), ('cluster', 'dp'))  68.6 us
    psum x2, blocking collectives, shards(): domain_prior = lax.psum(lax.psum(jnp.sum(joint, axis=0), 'dp'), 'cluster')  48.6 us
    psum x1, blocking collectives, shards(): row_total = lax.psum(jnp.sum(expo, axis=1), 'cluster')  18.2 us
    pmax x1, blocking collectives, shards(): row_max = lax.pmax(jnp.max(scores, axis=1), 'cluster')  16.6 us
    dot_general x1, matrix products, shards(): lax.dot_general(lax.all_gather(documents, 'cluster', axis=1, tiled=True),...  15.1 us
    dot_general x1, matrix products, shards(): lax.dot_general(columns, shares, (((0,), (0,)), ((), ())), preferred_elem...  9.11 us
  transfers between devices with their start and end apart: 2, of which 2 were waited for; matrix products, arithmetic and copies ran while one was open for 0% of the time, Pallas kernels for 0%

profile of v1, /device:TPU:1, one launch (start us, length us, event | category | flops | bytes accessed | tf_op | source)
XLA Modules:
  0.0 411.3 jit_solution(5762625800411717297)
XLA Ops:
  7.2 0.0 all-gather.2.cloned.1.call-start
  7.2 0.7 all-gather.2.cloned.1.call-update
  7.9 0.0 all-reduce.2.cloned.1.call-start
  7.9 1.9 reduce_sum.46
  9.9 77.0 %all-gather.2.cloned.1.call-done = bf16[2048,1024]{1,0:T(8,128)(2,1)} async-done(((bf16[2048,128]{1,0:T(8,128)(2,1)}), bf16[2048,1024]{1,0:T(8,128)(2,1)}) %all-gather.2.cloned.1.call-update) | async-done | bytes 4194320 | tf_op jit(solution)/shard_map/all_gather | solution.py:19
  86.9 15.1 %multiply_reduce_fusion = (f32[2048]{0:T(1024)S(1)}, f32[2048,2048]{0,1:T(8,128)}) fusion(bf16[2048,1024]{1,0:T(8,128)(2,1)} %all-gather.2.cloned.1.call-done, bf16[2048,1024]{1,0:T(8,128)(2,1)} %param.4), kind=kOutput, calls=%fused_computation.2 | convolution fusion | flops 8598321152 | bytes 25174016 | tf_op jit(solution)/shard_map/dot_general | solution.py:18
  102.0 16.6 %pmax.7 = f32[2048]{0:T(1024)S(1)} all-reduce(f32[2048]{0:T(1024)S(1)} %get-tuple-element.6), channel_id=1, replica_groups=mesh['cluster'=8,'dp'=16] {'cluster'}, use_global_device_ids=true, to_apply=%region_1.0 | all-reduce | flops 2048 | bytes 16384 | tf_op jit(solution)/shard_map/pmax | solution.py:26
  118.6 0.0 copy-start
  118.6 8.7 %fusion = f32[2048]{0:T(1024)S(1)} fusion(f32[2048,2048]{0,1:T(8,128)} %get-tuple-element.7, f32[2048]{0:T(1024)S(1)} %pmax.7), kind=kLoop, calls=%fused_computation.3 | loop fusion | flops 12580864 | bytes 16793600 | tf_op jit(solution)/shard_map/reduce_sum | solution.py:28
  127.3 18.2 %psum.35 = f32[2048]{0:T(1024)S(1)} all-reduce(f32[2048]{0:T(1024)S(1)} %fusion), channel_id=1, replica_groups=mesh['cluster'=8,'dp'=16] {'cluster'}, use_global_device_ids=true, to_apply=%region_3.0 | all-reduce | flops 2048 | bytes 16384 | tf_op jit(solution)/shard_map/psum | solution.py:28
  145.5 0.0 copy-done
  145.5 9.1 %fusion.1 = f32[2048,256]{1,0:T(8,128)} fusion(f32[2048,2048]{0,1:T(8,128)} %get-tuple-element.7, f32[2048]{0:T(1024)S(1)} %psum.35, f32[2048]{0:T(1024)S(1)} %pmax.7, f32[2048,256]{1,0:T(8,128)S(1)} %copy-done, f32[2048]{0:T(1024)S(1)} %reduce_sum.46), kind=kOutput, calls=%fused_computation.4 | convolution fusion | flops 2165309440 | bytes 20996096 | tf_op jit(solution)/shard_map/dot_general | solution.py:33
  154.6 0.0 all-reduce.2.cloned.1.call-update
  154.7 129.3 %all-reduce.2.cloned.1.call-done = f32[2048,256]{1,0:T(8,128)} async-done(((f32[2048,256]{1,0:T(8,128)}), f32[2048,256]{1,0:T(8,128)}) %all-reduce.2.cloned.1.call-update) | async-done | bytes 2097168 | tf_op jit(solution)/shard_map/psum | solution.py:32
  283.9 1.0 fusion.4
  284.9 28.3 %psum.37 = f32[256]{0:T(256)S(1)} all-reduce(f32[256]{0:T(256)S(1)} %get-tuple-element.3), channel_id=1, replica_groups=mesh['cluster'=8,'dp'=16] {'dp'}, use_global_device_ids=true, to_apply=%region_8.0 | all-reduce | flops 256 | bytes 2048 | tf_op jit(solution)/shard_map/psum | solution.py:41
  313.2 20.3 %psum.38 = f32[256]{0:T(256)S(1)} all-reduce(f32[256]{0:T(256)S(1)} %psum.37), channel_id=1, replica_groups=mesh['cluster'=8,'dp'=16] {'cluster'}, use_global_device_ids=true, to_apply=%region_9.0 | all-reduce | flops 256 | bytes 2048 | tf_op jit(solution)/shard_map/psum | solution.py:41
  333.5 2.3 multiply_reduce_fusion.1
  335.8 68.6 %psum.39 = f32[]{:T(128)} all-reduce(f32[]{:T(128)} %get-tuple-element.4), channel_id=1, replica_groups=mesh['cluster'=8,'dp'=16] {'cluster','dp'}, use_global_device_ids=true, to_apply=%region_11.0 | all-reduce | flops 1 | bytes 8 | tf_op jit(solution)/shard_map/psum | solution.py:43
Async XLA Ops:
  7.2 79.7 %all-gather.2.cloned.1.call-start = ((), (), s32[]{:S(2)}) async-start(), calls=%async_computation | async-start | bytes 4718592 | tf_op jit(solution)/shard_map/all_gather | solution.py:19
  7.9 276.0 %all-reduce.2.cloned.1.call-start = ((), (), s32[]{:S(2)}) async-start(), calls=%async_computation.1 | async-start | bytes 4194304 | tf_op jit(solution)/shard_map/psum | solution.py:32
  118.6 26.9 %copy-start = (f32[2048,256]{1,0:T(8,128)S(1)}, f32[2048,256]{1,0:T(8,128)}, u32[]{:S(2)}) copy-start(f32[2048,256]{1,0:T(8,128)} %param.5) | copy-start | bytes 6291460
Sparse Core Ops, SparseCore 0:
  10.2 76.6 all-gather.1
  154.8 129.0 all-reduce.1
